TPU v7x, 512 devices: a whole 4x4x16 slice. The times are simulated.
512 devices in a mesh: group: 16 (over x, y), dom: 32 (over z, core).
Axes of the slice: x: 4, y: 4, z: 16, core: 2. Of those that a mesh axis runs over, the one named last changes fastest.
Arguments:
- cell_dofs: float32 [9, 56, 131072], P(None, None, ('group', 'dom')), may hold values from -6 to 6
- star_matrix: float32 [3, 9, 9, 131072], P(None, None, None, ('group', 'dom')), may hold values from -1.8 to 1.8
- stiffness: float32 [3, 56, 56], replicated, may hold values from -0.75 to 0.75
- volume_kernel: float32 [3, 56, 56], replicated, may hold values from -0.75 to 0.75
- flux_local: float32 [4, 9, 9, 131072], P(None, None, None, ('group', 'dom')), may hold values from -0.9 to 0.9
- flux_neigh: float32 [4, 9, 9, 131072], P(None, None, None, ('group', 'dom')), may hold values from -0.9 to 0.9
- face_proj: float32 [4, 21, 56], replicated, may hold values from -0.75 to 0.75
- face_lift: float32 [4, 56, 21], replicated, may hold values from -1.25 to 1.25
- face_perm: float32 [3, 21, 21], replicated, may hold values from -1.25 to 1.25
- point_proj: float32 [4, 49, 56], replicated, may hold values from -0.75 to 0.75
- point_lift: float32 [4, 56, 49], replicated, may hold values from -0.875 to 0.875
- neighbour: int32 [4, 131072], P(None, ('group', 'dom')), may hold values from 0 to 351
- face_code: int32 [4, 131072], P(None, ('group', 'dom')), may hold values from 0 to 11
- send_near: int32 [2048, 16], P(('group', 'dom')), may hold values from 0 to 255
- send_strike: int32 [1024, 16], P(('group', 'dom')), may hold values from 0 to 255
- fault_minus: int32 [65536], P(('group', 'dom')), may hold values from 0 to 1023
- fault_send: int32 [2560, 32], P(('group', 'dom')), may hold values from 0 to 1023, as said below
- fault_plus: int32 [65536], P(('group', 'dom')), may hold values from 0 to 639, as said below
- fault_live: int32 [16, 32], P('group', 'dom'), may hold values from 1 to 128, 1536 in all within a row
- normal_load: float32 [65536], P(('group', 'dom')), may hold values from 1 to 8
- shear_load: float32 [65536], P(('group', 'dom')), may hold values from -4 to 4
- direct_effect: float32 [65536], P(('group', 'dom')), may hold values from 0.2 to 0.6
- state_var: float32 [65536], P(('group', 'dom')), may hold values from 0 to 1.5
Outputs:
- new_dofs: float32 [9, 56, 131072], P(None, None, ('group', 'dom'))
- slip_rate: float32 [6, 49, 65536], P(None, None, ('group', 'dom'))
Inputs may be any that keep to these rules, and one draw needn't show every extreme that they name: `fault_send`: each entry is a cell times 4 plus its fault face; the last entry of every list is cell 256 - 1 through face 3. The face in fault_plus equals the face of the list entry that it names; a slot names only lists whose sending partition lies inside the group; the share of slots per offset differs from partition to partition, and offset 0 means a far side in the same partition. `fault_live`: slots below this count are live, the others are empty.
All inputs are finite; a program needn't handle non-finite values. No bound on the sum of `fault_live` on one device may be relied on, other than what follows from the above.
Results may differ from a plain program's by a relative error of at most 0.0003.
Values sent between devices are 32-bit elements; how exact they have to be, the bound alone decides.
A program may use at most 128 MiB of HBM per device.

v0:
```python
import functools
import math

import jax
import jax.numpy as jnp
import numpy as np
from jax import lax
from jax.experimental import pallas as pl
from jax.experimental.pallas import tpu as pltpu
from jax.sharding import PartitionSpec as P

Q = 9
B = 56
FB = 21
FP = 24
NP = 49
NT = 6
NDER = 6
NEWTON = 4
N = 256
SLOTS = 128
LIST = 32
HALO = 16
FROWS = 13 * B
f32 = jnp.float32
bf16 = jnp.bfloat16
i32 = jnp.int32

GAUSS_POINTS = np.array(
    [
        -0.932469514203152,
        -0.6612093864662645,
        -0.2386191860831909,
        0.2386191860831909,
        0.6612093864662645,
        0.932469514203152,
    ]
)
GAUSS_MASSES = np.array(
    [
        0.1713244923791704,
        0.3607615730481386,
        0.467913934572691,
        0.467913934572691,
        0.3607615730481386,
        0.1713244923791704,
    ]
)
NODES = 0.5 * (GAUSS_POINTS + 1.0)
POWERS = [[float(NODES[t] ** k / math.factorial(k)) for k in range(NDER)] for t in range(NT)]
MASSES = [float(0.5 * w) for w in GAUSS_MASSES]
FAULT_OFFSETS = (-2, -1, 0, 1, 2)
NEAR_OFFSETS = (-2, -1, 1, 2)
STRIKE_OFFSETS = (-1, 1)

INPUTS = (
    ["cell", "star", "stiff", "volk", "fl", "fn", "proj", "lift", "perm", "pproj", "plift"]
    + ["neigh", "code", "near", "strike", "fminus", "fsend", "fplus", "live"]
    + ["nload", "sload", "deff", "svar"]
)
SCRATCH = dict(
    d0=pltpu.VMEM((NDER, 5, B, N), f32),
    d1=pltpu.VMEM((NDER, 5, B, N), f32),
    y0=pltpu.VMEM((5, 3 * B, N), f32),
    y1=pltpu.VMEM((5, 3 * B, N), f32),
    v0=pltpu.VMEM((Q, 3 * B + 4 * FP, 128), f32),
    v1=pltpu.VMEM((Q, 3 * B + 4 * FP, 128), f32),
    ig=pltpu.VMEM((Q * B, N), f32),
    lf=pltpu.VMEM((Q, B, N), f32),
    so=pltpu.VMEM((Q, 4 * FP, N), f32),
    ori=pltpu.VMEM((Q, 4 * FP, N), f32),
    a=pltpu.VMEM((NDER, 3 * B, N), f32),
    gm=pltpu.VMEM((NDER, 3 * B, SLOTS), f32),
    pk=pltpu.VMEM((NDER, 2 * B, SLOTS), f32),
    town=pltpu.VMEM((Q * 2 * FP, 4 * N), bf16),
    thalo=pltpu.VMEM((Q * 2 * FP, 4 * 128), bf16),
    pick=pltpu.VMEM((4, Q * 2 * FP, N), f32),
    z=pltpu.VMEM((8, B, N), f32),
    hs=pltpu.VMEM((96, 512), f32),
    hr=pltpu.VMEM((128, 512), f32),
    fs=pltpu.VMEM((NDER, 160, 128), f32),
    fr=pltpu.VMEM((NDER, 160, 128), f32),
    bs=pltpu.VMEM((160, 128), f32),
    br=pltpu.VMEM((256, 128), f32),
    wf=pltpu.VMEM((3 * B + 4 * FP, 384), f32),
    w1=pltpu.VMEM((3 * B, 3 * B), bf16),
    w2=pltpu.VMEM((3 * B + 4 * FP, 3 * B), bf16),
    wp=pltpu.VMEM((3 * FP, 3 * FP), bf16),
    wl=pltpu.VMEM((B, 12 * FP), bf16),
    wq=pltpu.VMEM((4 * B, 3 * B), bf16),
    wz=pltpu.VMEM((4 * B, 3 * B), bf16),
    in_sem=pltpu.SemaphoreType.DMA((23,)),
    fault_send_sem=pltpu.SemaphoreType.DMA((NDER, 4)),
    fault_recv_sem=pltpu.SemaphoreType.DMA((NDER, 4)),
    send_sem=pltpu.SemaphoreType.DMA((10,)),
    recv_sem=pltpu.SemaphoreType.DMA((10,)),
)


def rounded(x):
    return x.astype(bf16).astype(f32)


def split_rows(x):
    hi = rounded(x)
    return jnp.concatenate([hi, x - hi, hi], axis=0).astype(bf16)


def halves(x):
    hi = x.astype(bf16)
    return hi, (x - hi.astype(f32)).astype(bf16)


def dot(a, b):
    return jnp.dot(a, b, preferred_element_type=f32)


def dot_nt(a, b):
    return lax.dot_general(a, b, (((1,), (1,)), ((), ())), preferred_element_type=f32)


def iota(shape, dim):
    return lax.broadcasted_iota(i32, shape, dim)


def onehot(cond):
    return jnp.where(cond, 1.0, 0.0).astype(bf16)


def column(row):
    return jnp.broadcast_to(row.astype(f32), (128, 128)).T.astype(i32)


def wide(x):
    return jnp.concatenate([x, x], axis=1)


def put3(ref, row, cols, x):
    hi = rounded(x)
    lo = x - hi
    for c, part in zip(cols, (hi, hi, lo)):
        ref[row : row + x.shape[0], c : c + x.shape[1]] = part


def weave(*groups):
    steps = []
    for group in groups:
        steps += [((n + 0.5) / len(group), step) for n, step in enumerate(group)]
    for place, step in sorted(steps, key=lambda item: item[0]):
        step()


def mix27(star, tile, half, emit):
    lanes = slice(half * 128, half * 128 + 128)
    tiles = [[tile(j, q) for q in range(Q)] for j in range(3)]
    for p in range(Q):
        parts = []
        for j in range(3):
            acc = star[p, 0, j : j + 1, lanes] * tiles[j][0]
            for q in range(1, Q):
                acc = acc + star[p, q, j : j + 1, lanes] * tiles[j][q]
            parts.append(acc)
        emit(p, lanes, (parts[0] + parts[1]) + parts[2])


def mix9(flux, i, half, tile, dst, row, add):
    lanes = slice(half * 128, half * 128 + 128)
    tiles = [tile(q) for q in range(Q)]
    for p in range(Q):
        acc = flux[p, 0, i : i + 1, lanes] * tiles[0]
        for q in range(1, Q):
            acc = acc + flux[p, q, i : i + 1, lanes] * tiles[q]
        if add:
            acc = acc + dst[p, row : row + 8, lanes]
        dst[p, row : row + 8, lanes] = acc


def kernel(n_group, n_dom, *refs):
    names = ["u", "sl"] + INPUTS + list(SCRATCH)
    hbm = dict(zip(INPUTS, refs))
    r = dict(zip(names, refs[len(INPUTS) :]))
    cell, star, fl, fn = (r[k] for k in ("cell", "star", "fl", "fn"))
    dh, yh, vh = (r["d0"], r["d1"]), (r["y0"], r["y1"]), (r["v0"], r["v1"])
    ig, u, lf, so, ori, a = (r[k] for k in ("ig", "u", "lf", "so", "ori", "a"))
    gm, pk, town, thalo, pick, z = (r[k] for k in ("gm", "pk", "town", "thalo", "pick", "z"))
    hs, hr, fs, fr, bs, br = (r[k] for k in ("hs", "hr", "fs", "fr", "bs", "br"))
    wf, w1, w2, wp, wl, wq, wz = (r[k] for k in ("wf", "w1", "w2", "wp", "wl", "wq", "wz"))
    sl = r["sl"]
    g = lax.axis_index("group")
    me = lax.axis_index("dom")

    first = ["stiff", "cell", "star"]
    late = ["fl", "fn"]
    order = first + [name for name in INPUTS if name not in first + late] + late
    loads = {
        name: pltpu.make_async_copy(hbm[name], r[name], r["in_sem"].at[n])
        for n, name in enumerate(order)
    }
    for name in order:
        loads[name].start()

    def inside(axis, offset):
        at, size = (me, n_dom) if axis == "dom" else (g, n_group)
        target = at + offset
        return jnp.logical_and(target >= 0, target < size), target

    partners = [("dom", o) for o in NEAR_OFFSETS] + [("group", o) for o in STRIKE_OFFSETS]

    barrier = pltpu.get_barrier_semaphore()
    count = 0
    for axis, o in partners:
        ok, target = inside(axis, o)
        count = count + ok.astype(i32)

        @pl.when(ok)
        def _():
            pl.semaphore_signal(
                barrier,
                inc=1,
                device_id={axis: target},
                device_id_type=pl.DeviceIdType.MESH,
            )

    lists = [(s, slice(k * LIST, (k + 1) * LIST), FAULT_OFFSETS[k]) for s, k in enumerate((0, 1, 3, 4))]
    own_list = slice(2 * LIST, 3 * LIST)

    def fault_moves(k):
        return [
            (fs.at[k, rows], fr.at[k, rows], r["fault_send_sem"].at[k, s], r["fault_recv_sem"].at[k, s], "dom", o)
            for s, rows, o in lists
        ]

    halo_moves = []
    for s, (axis, o) in enumerate(partners):
        rows = slice(s * HALO, (s + 1) * HALO)
        halo_moves.append((hs.at[rows], hr.at[rows], r["send_sem"].at[s], r["recv_sem"].at[s], axis, o))
    back_moves = [
        (bs.at[rows], br.at[rows], r["send_sem"].at[6 + s], r["recv_sem"].at[6 + s], "dom", -o)
        for s, rows, o in lists
    ]

    def each(which, action):
        for src, dst, sent, got, axis, o in which:
            ok, target = inside(axis, -o if action == "wait_recv" else o)

            @pl.when(ok)
            def _():
                copy = pltpu.make_async_remote_copy(
                    src_ref=src,
                    dst_ref=dst,
                    send_sem=sent,
                    recv_sem=got,
                    device_id={axis: target},
                    device_id_type=pl.DeviceIdType.MESH,
                )
                getattr(copy, action)()

    for name in order:
        if name not in first + late:
            loads[name].wait()

    sends = r["fsend"][...]
    send_row = [
        jnp.concatenate([sends[k : k + 1, :] for k in range(4)], axis=1),
        jnp.concatenate([sends[4:5, :], jnp.full((1, 96), -4, i32)], axis=1),
    ]
    send_col = jnp.concatenate([column(row) for row in send_row], axis=0)[0:160]
    send_row = jnp.concatenate(send_row, axis=1)
    near = r["near"][...]
    strike = r["strike"][...]
    halo_row = jnp.concatenate(
        [near[k : k + 1, :] for k in range(4)]
        + [strike[k : k + 1, :] for k in range(2)]
        + [jnp.full((1, 32), -1, i32)],
        axis=1,
    )
    halo_col = column(halo_row)[0:96]
    minus_row = r["fminus"][...]
    minus_col = column(minus_row)
    plus_row = r["fplus"][...]
    plus_col = column(lax.shift_right_logical(plus_row, 2))
    send_hot = onehot(lax.shift_right_arithmetic(wide(send_col), 2) == iota((160, N), 1))
    halo_hot = onehot(wide(halo_col) == iota((96, N), 1))
    minus_hot = onehot(lax.shift_right_logical(minus_row, 2) == iota((N, SLOTS), 0))
    plus_hot = onehot(wide(plus_col)[:, 0:160] == iota((SLOTS, 160), 1))
    codes = r["code"][...]
    faces = (codes >= 3).astype(i32) + (codes >= 6).astype(i32) + (codes >= 9).astype(i32)
    turns = codes - 3 * faces
    keys = faces * 384 + r["neigh"][...]

    loads["stiff"].wait()
    put3(wf, 0, (0, 56, 112), jnp.concatenate([r["stiff"][j].T for j in range(3)], axis=0))
    w1[...] = wf[0 : 3 * B, 0 : 3 * B].astype(bf16)
    put3(wf, 0, (0, 56, 112), jnp.concatenate([r["volk"][j].T for j in range(3)], axis=0))
    wf[3 * B :, 0 : 3 * B] = jnp.zeros((4 * FP, 3 * B), f32)
    for i in range(4):
        put3(wf, 3 * B + FP * i, (0, 56, 112), r["proj"][:, i, :])
    w2[...] = wf[:, 0 : 3 * B].astype(bf16)
    wf[...] = jnp.zeros_like(wf)
    for h in range(3):
        put3(wf, FP * h, (0, FP, 2 * FP), r["perm"][h])
    wp[...] = wf[0 : 3 * FP, 0 : 3 * FP].astype(bf16)
    wf[...] = jnp.zeros_like(wf)
    for i in range(4):
        put3(wf, 0, tuple(FP * (i + 4 * s) for s in range(3)), r["lift"][:, i, :].T)
    wl[...] = wf[0:B, 0 : 12 * FP].astype(bf16)
    wf[...] = jnp.zeros_like(wf)
    for i in range(4):
        put3(wf, B * i, (0, 56, 112), r["pproj"][:, i, :])
    wq[...] = wf[0 : 4 * B, 0 : 3 * B].astype(bf16)
    wf[...] = jnp.zeros_like(wf)
    for i in range(4):
        put3(wf, B * i, (0, 56, 112), r["plift"][:, i, :].T)
    wz[...] = wf[0 : 4 * B, 0 : 3 * B].astype(bf16)

    for s, rows, o in lists:
        for ref, offset in ((fr, o), (br, -o)):
            ok, target = inside("dom", -offset)

            @pl.when(jnp.logical_not(ok))
            def _():
                if ref is fr:
                    for k in range(NDER):
                        fr[k, rows] = jnp.zeros((LIST, 128), f32)
                else:
                    br[rows] = jnp.zeros((LIST, 128), f32)

    for s, (axis, o) in enumerate(partners):
        ok, target = inside(axis, -o)

        @pl.when(jnp.logical_not(ok))
        def _():
            hr[s * HALO : (s + 1) * HALO] = jnp.zeros((HALO, 512), f32)

    hr[96:128, :] = jnp.zeros((32, 512), f32)
    br[160:256, :] = jnp.zeros((96, 128), f32)

    loads["cell"].wait()
    for q in range(Q):
        value = cell[q]
        ig[q * B : (q + 1) * B, :] = value
        for half in range(2):
            dh[half][0, q // 2, :, (q % 2) * 128 : (q % 2) * 128 + 128] = value[
                :, half * 128 : half * 128 + 128
            ]
    a[0, 0:B] = cell[0]
    a[0, B : 2 * B] = cell[3] + cell[7]
    a[0, 2 * B :] = cell[3] - cell[7]
    loads["star"].wait()

    def moved(k, half):
        def one(pair):
            width = 256 if pair < 4 else 128
            yh[half][pair, :, 0:width] = dot(w1[...], split_rows(dh[half][k, pair, :, 0:width]))

        return [functools.partial(one, pair) for pair in range(5)]

    def mixed(k, half, weight):
        def one(ct):
            held = {}

            def tile(j, q):
                row = j * B + ct * 8
                lane = (q % 2) * 128
                return yh[half][q // 2, row : row + 8, lane : lane + 128]

            def emit(p, lanes, value):
                rows = slice(ct * 8, ct * 8 + 8)
                lane = (p % 2) * 128
                dh[half][k + 1, p // 2, rows, lane : lane + 128] = value
                at = slice(p * B + ct * 8, p * B + ct * 8 + 8)
                ig[at, lanes] = ig[at, lanes] + value * weight
                if p == 0:
                    a[k + 1, rows, lanes] = value
                if p == 3:
                    held[0] = value
                if p == 7:
                    at = slice(B + ct * 8, B + ct * 8 + 8)
                    a[k + 1, at, lanes] = held[0] + value
                    at = slice(2 * B + ct * 8, 2 * B + ct * 8 + 8)
                    a[k + 1, at, lanes] = held[0] - value

            mix27(star, tile, half, emit)

        return [functools.partial(one, ct) for ct in range(7)]

    def payload(k):
        hi, lo = halves(a[k])
        rows = 2 * B
        fs[k, :, 0:rows] = dot_nt(send_hot, hi[0:rows]) + dot_nt(send_hot, lo[0:rows])
        fs[k, :, rows:] = jnp.zeros((160, 128 - rows), f32)
        gm[k] = dot(hi, minus_hot) + dot(lo, minus_hot)

    def post(k):
        each(fault_moves(k), "start")
        fr[k, own_list] = fs[k, own_list]

    def derive(k, weight):
        weight = weight / (k + 2).astype(f32)
        payload(k)
        weave(moved(k, 1), mixed(k, 0, weight))

        @pl.when(k == 2)
        def _():
            pl.semaphore_wait(barrier, count)
            post(0)
            post(1)
            post(2)

        @pl.when(k == 3)
        def _():
            post(3)

        weave(moved(k + 1, 0), mixed(k, 1, weight))
        return weight

    def spread(half):
        lanes = slice(half * 128, half * 128 + 128)

        def one(q):
            vh[half][q] = dot(w2[...], split_rows(ig[q * B : (q + 1) * B, lanes]))

        return [functools.partial(one, q) for q in range(Q)]

    weave(moved(0, 0))
    lax.fori_loop(0, NDER - 2, derive, jnp.float32(1.0))
    last = NDER - 2
    weight = jnp.float32(1.0 / math.factorial(NDER))
    payload(last)
    weave(moved(last, 1), mixed(last, 0, weight))
    post(last)
    weave(spread(0), mixed(last, 1, weight))
    payload(last + 1)
    i_hi, i_lo = halves(ig[...])
    hs[:, 0 : Q * B] = dot_nt(halo_hot, i_hi) + dot_nt(halo_hot, i_lo)
    hs[:, Q * B : 512] = jnp.zeros((96, 512 - Q * B), f32)
    post(last + 1)
    each(halo_moves, "start")
    send_cells = lax.shift_right_arithmetic(send_row, 2)
    shear_hot = jnp.concatenate([onehot(send_cells == iota((N, 256), 0)), minus_hot], axis=1)
    s_hi, s_lo = i_hi[3 * B : 4 * B], i_lo[3 * B : 4 * B]
    face_row = jnp.concatenate([minus_row & 3, plus_row & 3], axis=1)

    def projected(x, row):
        full = dot(wq[...], split_rows(x))
        best = full[3 * B :]
        for i in range(3):
            best = jnp.where(row == i, full[i * B : (i + 1) * B], best)
        return best

    shear = projected(
        dot(s_hi, shear_hot) + dot(s_lo, shear_hot),
        jnp.concatenate([send_row & 3, minus_row & 3], axis=1),
    )
    psi, m_w = shear[:, 0:256], shear[:, 256:]

    loads["fl"].wait()

    def local(half):
        def inner(ct):
            def tile(j, q):
                row = j * B + ct * 8
                return vh[half][q, row : row + 8, :]

            def emit(p, lanes, value):
                rows = slice(ct * 8, ct * 8 + 8)
                u[p, rows, lanes] = cell[p, rows, lanes] + value

            mix27(star, tile, half, emit)

        def face(row):
            mix9(
                fl, row // FP, half, lambda q: vh[half][q, 3 * B + row : 3 * B + row + 8, :], so, row, False
            )

        return [functools.partial(inner, ct) for ct in range(7)] + [
            functools.partial(face, row) for row in range(0, 4 * FP, 8)
        ]

    def table(half):
        for q in range(Q):
            for j in range(4):
                block = vh[half][q, 3 * B + FP * j : 3 * B + FP * (j + 1), :]
                hi = rounded(block)
                town[
                    q * 2 * FP : (q + 1) * 2 * FP, j * N + half * 128 : j * N + half * 128 + 128
                ] = jnp.concatenate([hi, block - hi], axis=0).astype(bf16)

    def arrived(k):
        hi, lo = halves(fr[k])
        gt = (dot(plus_hot, hi) + dot(plus_hot, lo)).T
        for n in range(2):
            both = jnp.concatenate(
                [gm[k, 2 * n * B : 2 * n * B + B], gt[n * B : (n + 1) * B]], axis=1
            )
            best = projected(both, face_row)
            pk[k, n * B : (n + 1) * B] = best[:, 0:SLOTS] + best[:, SLOTS:]

    def near_pick(i):
        hot = jnp.concatenate(
            [onehot(keys[i : i + 1, :] == iota((N, N), 0) + 384 * j) for j in range(4)], axis=0
        )
        pick[i] = dot(town[...], hot)
    weave(local(0), spread(1))
    table(0)
    table(1)
    for k in range(NDER - 1):
        each(fault_moves(k), "wait_recv")
    weave(local(1), [functools.partial(arrived, k) for k in range(NDER - 1)] + [functools.partial(near_pick, i) for i in range(4)])

    each(fault_moves(NDER - 1), "wait_recv")
    each(halo_moves, "wait_recv")
    arrived(NDER - 1)
    alive = (iota((1, SLOTS), 1) < r["live"][...]).astype(f32)
    nload, sload, deff = r["nload"][...], r["sload"][...], r["deff"][...]
    factor = 0.5 * jnp.exp(r["svar"][...] / deff)
    total = jnp.zeros((B, SLOTS), f32)
    for t in range(NT):
        normal = pk[0, 0:B]
        tangent = pk[0, B:]
        for k in range(1, NDER):
            normal = normal + POWERS[t][k] * pk[k, 0:B]
            tangent = tangent + POWERS[t][k] * pk[k, B:]
        strength = jnp.maximum(nload - 0.5 * normal, 0.0)
        locked = sload + 0.5 * tangent
        scaled = strength * deff
        curve = scaled * factor
        now = locked / (0.5 + curve)
        for m in range(NEWTON - 1):
            arg = factor * now
            root = jnp.sqrt(1.0 + arg * arg)
            mag = jnp.log(jnp.abs(arg) + root)
            asinh = jnp.where(arg < 0, -mag, mag)
            residue = locked - 0.5 * now - scaled * asinh
            slope = -0.5 - curve / root
            now = now - residue / slope
        sl[t] = (now * alive)[0:NP]
        total = total + MASSES[t] * (locked - sload - 0.5 * now)
    am = (total - m_w) * alive
    ap = jnp.where(iota((B, SLOTS), 0) == NP, alive, total * alive)

    entry_hot = onehot(lax.shift_right_logical(plus_row, 2) == iota((160, SLOTS), 0))
    b_hi, b_lo = halves(jnp.concatenate([ap, jnp.zeros((128 - B, SLOTS), f32)], axis=0))
    bs[...] = dot_nt(entry_hot, b_hi) + dot_nt(entry_hot, b_lo)
    each(back_moves, "start")
    br[own_list, :] = bs[own_list, :]

    ht = hr[...].T
    for q in range(Q):
        full = dot(w2[3 * B :, :], split_rows(ht[q * B : (q + 1) * B, :]))
        for j in range(4):
            block = full[FP * j : FP * (j + 1), :]
            hi = rounded(block)
            thalo[q * 2 * FP : (q + 1) * 2 * FP, j * 128 : (j + 1) * 128] = jnp.concatenate(
                [hi, block - hi], axis=0
            ).astype(bf16)
    loads["fn"].wait()

    def turned(i):
        hot = jnp.concatenate(
            [onehot(keys[i : i + 1, :] == iota((128, N), 0) + (384 * j + N)) for j in range(4)],
            axis=0,
        )
        both = pick[i] + dot(thalo[...], hot)
        for q in range(Q):
            hi = both[q * 2 * FP : q * 2 * FP + FP]
            lo = both[q * 2 * FP + FP : (q + 1) * 2 * FP]
            full = dot(wp[...], jnp.concatenate([hi, lo, hi], axis=0).astype(bf16))
            best = full[2 * FP :]
            for h in range(2):
                best = jnp.where(turns[i : i + 1, :] == h, full[h * FP : (h + 1) * FP], best)
            ori[q, i * FP : (i + 1) * FP, :] = best

    def far(i):
        def one(row, half):
            lanes = slice(half * 128, half * 128 + 128)
            mix9(fn, i, half, lambda q: ori[q, row : row + 8, lanes], so, row, True)

        return [
            functools.partial(one, row, half)
            for row in range(i * FP, (i + 1) * FP, 8)
            for half in range(2)
        ]

    weave([functools.partial(turned, 0)])
    for i in range(3):
        weave([functools.partial(turned, i + 1)], far(i))

    each(back_moves, "wait_recv")
    am_hi, am_lo = halves(am)
    back = br[...].T
    back = back[0:B] - back[NP : NP + 1] * psi
    bt_hi, bt_lo = halves(back[:, 0:160])

    def lifted(i):
        own_hot = onehot(wide(minus_col) == iota((SLOTS, N), 1) * 4 + i)
        far_hot = onehot(wide(send_col) == iota((160, N), 1) * 4 + i)
        e_m = dot(am_hi, own_hot) + dot(am_lo, own_hot)
        e_p = dot(bt_hi, far_hot) + dot(bt_lo, far_hot)
        w = wz[i * B : (i + 1) * B, :]
        z[i] = dot(w, split_rows(e_m + e_p))
        z[4 + i] = dot(w, split_rows(e_m - e_p))

    weave([functools.partial(lifted, i) for i in range(4)], far(3))
    lf[0] = dot(wl[...], split_rows(so[0]))
    for p in range(Q):
        if p + 1 < Q:
            lf[p + 1] = dot(wl[...], split_rows(so[p + 1]))
        for ct in range(7):
            rows = slice(ct * 8, ct * 8 + 8)
            for half in range(2):
                lanes = slice(half * 128, half * 128 + 128)
                acc = u[p, rows, lanes] - lf[p, rows, lanes]
                for i in range(4):
                    acc = acc + fl[p, 3, i : i + 1, lanes] * z[i, rows, lanes]
                    acc = acc + fl[p, 7, i : i + 1, lanes] * z[4 + i, rows, lanes]
                u[p, rows, lanes] = acc
    for k in range(NDER):
        each(fault_moves(k), "wait_send")
    each(halo_moves, "wait_send")
    each(back_moves, "wait_send")


def per_device(n_group, n_dom, *args):
    args = list(args)
    for at in (1, 4, 5):
        args[at] = args[at].transpose(1, 2, 0, 3)
    for at in (6, 9):
        args[at] = args[at].transpose(1, 0, 2)
    for at in (7, 10):
        args[at] = args[at].transpose(2, 0, 1)
    for at in (15, 17, 19, 20, 21, 22):
        args[at] = args[at].reshape(1, SLOTS)
    return pl.pallas_call(
        functools.partial(kernel, n_group, n_dom),
        out_shape=(pltpu.VMEM((Q, B, N), f32), pltpu.VMEM((NT, NP, SLOTS), f32)),
        in_specs=[pl.BlockSpec(memory_space=pl.ANY)] * len(args),
        out_specs=(pl.BlockSpec(memory_space=pltpu.VMEM),) * 2,
        scratch_shapes=[pltpu.VMEM(x.shape, x.dtype) for x in args] + list(SCRATCH.values()),
        compiler_params=pltpu.CompilerParams(
            collective_id=0, has_side_effects=True, vmem_limit_bytes=56 << 20
        ),
        name="ader_step",
    )(*args)


def solution(mesh):
    both = ("group", "dom")
    return jax.shard_map(
        functools.partial(per_device, mesh.shape["group"], mesh.shape["dom"]),
        mesh=mesh,
        in_specs=(
            P(None, None, both),
            P(None, None, None, both),
            P(),
            P(),
            P(None, None, None, both),
            P(None, None, None, both),
            P(),
            P(),
            P(),
            P(),
            P(),
            P(None, both),
            P(None, both),
            P(both, None),
            P(both, None),
            P(both),
            P(both, None),
            P(both),
            P("group", "dom"),
            P(both),
            P(both),
            P(both),
            P(both),
        ),
        out_specs=(P(None, None, both), P(None, None, both)),
        check_vma=False,
    )
```

profile of v0, /device:TPU:1, one launch (start us, length us, event | category | flops | bytes accessed | tf_op | source)
XLA Modules:
  0.0 32.1 jit_solution(12309950071467023204)
XLA Ops:
  1.3 29.4 %ader_step.1 = (f32[9,56,256]{2,1,0:T(8,128)S(1)}, f32[6,49,128]{2,1,0:T(8,128)S(1)}) custom-call(f32[9,56,256]{2,1,0:T(8,128)} %refs_0_.1, f32[9,9,3,256]{3,2,1,0:T(4,128)} %bitcast.13, f32[3,56,56]{2,1,0:T(8,128)} %refs_2_.1, f32[3,56,56]{2,1,0:T(8,128)} %refs_3_.1, f32[9,9,4,256]{3,2,1,0:T(4,128)} %bitcast.14, f32[9,9,4,256]{3,2,1,0:T(4,128)} %bitcast.15, ...), custom_call_target="tpu_custom_call" | custom-call | tf_op jit(solution)/shard_map/ader_step/pallas_call | solution.py:634
  30.7 0.8 %copy.27 = f32[9,56,256]{2,1,0:T(8,128)} copy(f32[9,56,256]{2,1,0:T(8,128)S(1)} %get-tuple-element.2) | data formatting | bytes 1032192
  31.5 0.7 %copy.28 = f32[6,49,128]{2,1,0:T(8,128)} copy(f32[6,49,128]{2,1,0:T(8,128)S(1)} %get-tuple-element.3) | data formatting | bytes 301056
where the time goes:
time: 32.3 us; the launch traced here: 32.1 us
  Pallas kernels  29.4 us (91%)
  local copies, waits for them, and re-layouts  1.46 us (5%)
  between operations  1.29 us (4%)
    pallas_call x1, Pallas kernels, per_device(): pl.pallas_call(functools.partial(kernel, n_group, n_dom), out_shape=(pltp...  29.4 us
    unnamed x2, local copies, waits for them, and re-layouts  1.46 us

commit v1 on v0

--- a/solution.py
+++ b/solution.py
@@ -66,7 +66,6 @@
     v0=pltpu.VMEM((Q, 3 * B + 4 * FP, 128), f32),
     v1=pltpu.VMEM((Q, 3 * B + 4 * FP, 128), f32),
     ig=pltpu.VMEM((Q * B, N), f32),
-    lf=pltpu.VMEM((Q, B, N), f32),
     so=pltpu.VMEM((Q, 4 * FP, N), f32),
     ori=pltpu.VMEM((Q, 4 * FP, N), f32),
     a=pltpu.VMEM((NDER, 3 * B, N), f32),
@@ -90,8 +89,8 @@
     wq=pltpu.VMEM((4 * B, 3 * B), bf16),
     wz=pltpu.VMEM((4 * B, 3 * B), bf16),
     in_sem=pltpu.SemaphoreType.DMA((23,)),
-    fault_send_sem=pltpu.SemaphoreType.DMA((NDER, 4)),
-    fault_recv_sem=pltpu.SemaphoreType.DMA((NDER, 4)),
+    fault_send_sem=pltpu.SemaphoreType.DMA((2, 4)),
+    fault_recv_sem=pltpu.SemaphoreType.DMA((2, 4)),
     send_sem=pltpu.SemaphoreType.DMA((10,)),
     recv_sem=pltpu.SemaphoreType.DMA((10,)),
 )
@@ -181,7 +180,7 @@
     r = dict(zip(names, refs[len(INPUTS) :]))
     cell, star, fl, fn = (r[k] for k in ("cell", "star", "fl", "fn"))
     dh, yh, vh = (r["d0"], r["d1"]), (r["y0"], r["y1"]), (r["v0"], r["v1"])
-    ig, u, lf, so, ori, a = (r[k] for k in ("ig", "u", "lf", "so", "ori", "a"))
+    ig, u, so, ori, a = (r[k] for k in ("ig", "u", "so", "ori", "a"))
     gm, pk, town, thalo, pick, z = (r[k] for k in ("gm", "pk", "town", "thalo", "pick", "z"))
     hs, hr, fs, fr, bs, br = (r[k] for k in ("hs", "hr", "fs", "fr", "bs", "br"))
     wf, w1, w2, wp, wl, wq, wz = (r[k] for k in ("wf", "w1", "w2", "wp", "wl", "wq", "wz"))
@@ -189,9 +188,8 @@
     g = lax.axis_index("group")
     me = lax.axis_index("dom")
 
-    first = ["stiff", "cell", "star"]
-    late = ["fl", "fn"]
-    order = first + [name for name in INPUTS if name not in first + late] + late
+    large = ["cell", "star", "fl", "fn"]
+    order = [name for name in INPUTS if name not in large] + large
     loads = {
         name: pltpu.make_async_copy(hbm[name], r[name], r["in_sem"].at[n])
         for n, name in enumerate(order)
@@ -224,9 +222,17 @@
     lists = [(s, slice(k * LIST, (k + 1) * LIST), FAULT_OFFSETS[k]) for s, k in enumerate((0, 1, 3, 4))]
     own_list = slice(2 * LIST, 3 * LIST)
 
-    def fault_moves(k):
+    def fault_moves(part):
+        orders = (slice(0, 4), slice(4, NDER))[part]
         return [
-            (fs.at[k, rows], fr.at[k, rows], r["fault_send_sem"].at[k, s], r["fault_recv_sem"].at[k, s], "dom", o)
+            (
+                fs.at[orders, rows],
+                fr.at[orders, rows],
+                r["fault_send_sem"].at[part, s],
+                r["fault_recv_sem"].at[part, s],
+                "dom",
+                o,
+            )
             for s, rows, o in lists
         ]
 
@@ -240,23 +246,28 @@
     ]
 
     def each(which, action):
-        for src, dst, sent, got, axis, o in which:
-            ok, target = inside(axis, -o if action == "wait_recv" else o)
+        for axis, o in partners:
+            to = -o if action == "wait_recv" else o
+            ok, target = inside(axis, to)
+            mine = [move for move in which if move[4:] == (axis, o)]
+            if not mine:
+                continue
 
             @pl.when(ok)
             def _():
-                copy = pltpu.make_async_remote_copy(
-                    src_ref=src,
-                    dst_ref=dst,
-                    send_sem=sent,
-                    recv_sem=got,
-                    device_id={axis: target},
-                    device_id_type=pl.DeviceIdType.MESH,
-                )
-                getattr(copy, action)()
+                for src, dst, sent, got, _, _ in mine:
+                    copy = pltpu.make_async_remote_copy(
+                        src_ref=src,
+                        dst_ref=dst,
+                        send_sem=sent,
+                        recv_sem=got,
+                        device_id={axis: target},
+                        device_id_type=pl.DeviceIdType.MESH,
+                    )
+                    getattr(copy, action)()
 
     for name in order:
-        if name not in first + late:
+        if name not in large:
             loads[name].wait()
 
     sends = r["fsend"][...]
@@ -286,9 +297,16 @@
     codes = r["code"][...]
     faces = (codes >= 3).astype(i32) + (codes >= 6).astype(i32) + (codes >= 9).astype(i32)
     turns = codes - 3 * faces
-    keys = faces * 384 + r["neigh"][...]
-
-    loads["stiff"].wait()
+    near_col = r["neigh"][...]
+
+    def masked(hot, i):
+        parts = [
+            hot * jnp.broadcast_to(jnp.where(faces[i : i + 1, :] == j, 1.0, 0.0), hot.shape).astype(bf16)
+            for j in range(4)
+        ]
+        return jnp.concatenate(parts, axis=0)
+
+
     put3(wf, 0, (0, 56, 112), jnp.concatenate([r["stiff"][j].T for j in range(3)], axis=0))
     w1[...] = wf[0 : 3 * B, 0 : 3 * B].astype(bf16)
     put3(wf, 0, (0, 56, 112), jnp.concatenate([r["volk"][j].T for j in range(3)], axis=0))
@@ -390,9 +408,6 @@
         fs[k, :, 0:rows] = dot_nt(send_hot, hi[0:rows]) + dot_nt(send_hot, lo[0:rows])
         fs[k, :, rows:] = jnp.zeros((160, 128 - rows), f32)
         gm[k] = dot(hi, minus_hot) + dot(lo, minus_hot)
-
-    def post(k):
-        each(fault_moves(k), "start")
         fr[k, own_list] = fs[k, own_list]
 
     def derive(k, weight):
@@ -400,16 +415,10 @@
         payload(k)
         weave(moved(k, 1), mixed(k, 0, weight))
 
-        @pl.when(k == 2)
+        @pl.when(k == 3)
         def _():
             pl.semaphore_wait(barrier, count)
-            post(0)
-            post(1)
-            post(2)
-
-        @pl.when(k == 3)
-        def _():
-            post(3)
+            each(fault_moves(0), "start")
 
         weave(moved(k + 1, 0), mixed(k, 1, weight))
         return weight
@@ -428,14 +437,12 @@
     weight = jnp.float32(1.0 / math.factorial(NDER))
     payload(last)
     weave(moved(last, 1), mixed(last, 0, weight))
-    post(last)
     weave(spread(0), mixed(last, 1, weight))
     payload(last + 1)
     i_hi, i_lo = halves(ig[...])
     hs[:, 0 : Q * B] = dot_nt(halo_hot, i_hi) + dot_nt(halo_hot, i_lo)
     hs[:, Q * B : 512] = jnp.zeros((96, 512 - Q * B), f32)
-    post(last + 1)
-    each(halo_moves, "start")
+    each(fault_moves(1) + halo_moves, "start")
     send_cells = lax.shift_right_arithmetic(send_row, 2)
     shear_hot = jnp.concatenate([onehot(send_cells == iota((N, 256), 0)), minus_hot], axis=1)
     s_hi, s_lo = i_hi[3 * B : 4 * B], i_lo[3 * B : 4 * B]
@@ -497,20 +504,17 @@
             pk[k, n * B : (n + 1) * B] = best[:, 0:SLOTS] + best[:, SLOTS:]
 
     def near_pick(i):
-        hot = jnp.concatenate(
-            [onehot(keys[i : i + 1, :] == iota((N, N), 0) + 384 * j) for j in range(4)], axis=0
-        )
+        hot = masked(onehot(near_col[i : i + 1, :] == iota((N, N), 0)), i)
         pick[i] = dot(town[...], hot)
     weave(local(0), spread(1))
     table(0)
     table(1)
-    for k in range(NDER - 1):
-        each(fault_moves(k), "wait_recv")
-    weave(local(1), [functools.partial(arrived, k) for k in range(NDER - 1)] + [functools.partial(near_pick, i) for i in range(4)])
-
-    each(fault_moves(NDER - 1), "wait_recv")
-    each(halo_moves, "wait_recv")
-    arrived(NDER - 1)
+    each(fault_moves(0), "wait_recv")
+    weave(local(1), [functools.partial(arrived, k) for k in range(4)] + [functools.partial(near_pick, i) for i in range(4)])
+
+    each(fault_moves(1) + halo_moves, "wait_recv")
+    arrived(4)
+    arrived(5)
     alive = (iota((1, SLOTS), 1) < r["live"][...]).astype(f32)
     nload, sload, deff = r["nload"][...], r["sload"][...], r["deff"][...]
     factor = 0.5 * jnp.exp(r["svar"][...] / deff)
@@ -557,10 +561,7 @@
     loads["fn"].wait()
 
     def turned(i):
-        hot = jnp.concatenate(
-            [onehot(keys[i : i + 1, :] == iota((128, N), 0) + (384 * j + N)) for j in range(4)],
-            axis=0,
-        )
+        hot = masked(onehot(near_col[i : i + 1, :] == iota((128, N), 0) + N), i)
         both = pick[i] + dot(thalo[...], hot)
         for q in range(Q):
             hi = both[q * 2 * FP : q * 2 * FP + FP]
@@ -586,39 +587,48 @@
     for i in range(3):
         weave([functools.partial(turned, i + 1)], far(i))
 
+    am_hi, am_lo = halves(am)
+
+    def own_lift(i):
+        own_hot = onehot(wide(minus_col) == iota((SLOTS, N), 1) * 4 + i)
+        e_m = dot(am_hi, own_hot) + dot(am_lo, own_hot)
+        z[i] = dot(wz[i * B : (i + 1) * B, :], split_rows(e_m))
+
+    def lift(p):
+        u[p] = u[p] - dot(wl[...], split_rows(so[p]))
+
+    weave([functools.partial(own_lift, i) for i in range(4)], far(3))
+    far_hot = [onehot(wide(send_col) == iota((160, N), 1) * 4 + i) for i in range(4)]
+    weave([functools.partial(lift, p) for p in range(Q)])
+
     each(back_moves, "wait_recv")
-    am_hi, am_lo = halves(am)
     back = br[...].T
     back = back[0:B] - back[NP : NP + 1] * psi
     bt_hi, bt_lo = halves(back[:, 0:160])
-
-    def lifted(i):
-        own_hot = onehot(wide(minus_col) == iota((SLOTS, N), 1) * 4 + i)
-        far_hot = onehot(wide(send_col) == iota((160, N), 1) * 4 + i)
-        e_m = dot(am_hi, own_hot) + dot(am_lo, own_hot)
-        e_p = dot(bt_hi, far_hot) + dot(bt_lo, far_hot)
-        w = wz[i * B : (i + 1) * B, :]
-        z[i] = dot(w, split_rows(e_m + e_p))
-        z[4 + i] = dot(w, split_rows(e_m - e_p))
-
-    weave([functools.partial(lifted, i) for i in range(4)], far(3))
-    lf[0] = dot(wl[...], split_rows(so[0]))
-    for p in range(Q):
-        if p + 1 < Q:
-            lf[p + 1] = dot(wl[...], split_rows(so[p + 1]))
-        for ct in range(7):
-            rows = slice(ct * 8, ct * 8 + 8)
-            for half in range(2):
-                lanes = slice(half * 128, half * 128 + 128)
-                acc = u[p, rows, lanes] - lf[p, rows, lanes]
+    for i in range(4):
+        e_p = dot(bt_hi, far_hot[i]) + dot(bt_lo, far_hot[i])
+        z_p = dot(wz[i * B : (i + 1) * B, :], split_rows(e_p))
+        z_m = z[i]
+        z[i] = z_m + z_p
+        z[4 + i] = z_m - z_p
+
+    def finish(n, carry):
+        at = pl.multiple_of(n * 8, 8)
+        rows = pl.ds(at, 8)
+        for half in range(2):
+            lanes = slice(half * 128, half * 128 + 128)
+            tiles = [z[i, rows, lanes] for i in range(8)]
+            for p in range(Q):
+                acc = u[p, rows, lanes]
                 for i in range(4):
-                    acc = acc + fl[p, 3, i : i + 1, lanes] * z[i, rows, lanes]
-                    acc = acc + fl[p, 7, i : i + 1, lanes] * z[4 + i, rows, lanes]
+                    acc = acc + (
+                        fl[p, 3, i : i + 1, lanes] * tiles[i] + fl[p, 7, i : i + 1, lanes] * tiles[4 + i]
+                    )
                 u[p, rows, lanes] = acc
-    for k in range(NDER):
-        each(fault_moves(k), "wait_send")
-    each(halo_moves, "wait_send")
-    each(back_moves, "wait_send")
+        return carry
+
+    lax.fori_loop(0, 7, finish, 0)
+    each(fault_moves(0) + fault_moves(1) + halo_moves + back_moves, "wait_send")
 
 
 def per_device(n_group, n_dom, *args):

time: 32.3 us -> 30.3 us (0.938)
  Pallas kernels: 29.4 us -> 27.4 us
    pallas_call x1, Pallas kernels: 29.4 us -> 27.4 us  [per_device(): pl.pallas_call(functools.partial(kernel, n_group, n_dom), out_shape=(pltp...]
where the time goes in v1:
time: 30.3 us; the launch traced here: 30.2 us
  Pallas kernels  27.4 us (90%)
  local copies, waits for them, and re-layouts  1.46 us (5%)
  between operations  1.29 us (4%)
    pallas_call x1, Pallas kernels, per_device(): pl.pallas_call(functools.partial(kernel, n_group, n_dom), out_shape=(pltp...  27.4 us
    unnamed x2, local copies, waits for them, and re-layouts  1.46 us

profile of v1, /device:TPU:1, one launch (start us, length us, event | category | flops | bytes accessed | tf_op | source)
XLA Modules:
  0.0 30.2 jit_solution(14481856634957090906)
XLA Ops:
  1.3 27.4 %ader_step.1 = (f32[9,56,256]{2,1,0:T(8,128)S(1)}, f32[6,49,128]{2,1,0:T(8,128)S(1)}) custom-call(f32[9,56,256]{2,1,0:T(8,128)} %refs_0_.1, f32[9,9,3,256]{3,2,1,0:T(4,128)} %bitcast.13, f32[3,56,56]{2,1,0:T(8,128)} %refs_2_.1, f32[3,56,56]{2,1,0:T(8,128)} %refs_3_.1, f32[9,9,4,256]{3,2,1,0:T(4,128)} %bitcast.14, f32[9,9,4,256]{3,2,1,0:T(4,128)} %bitcast.15, ...), custom_call_target="tpu_custom_call" | custom-call | tf_op jit(solution)/shard_map/ader_step/pallas_call | solution.py:644
  28.7 0.8 %copy.27 = f32[9,56,256]{2,1,0:T(8,128)} copy(f32[9,56,256]{2,1,0:T(8,128)S(1)} %get-tuple-element.2) | data formatting | bytes 1032192
  29.5 0.7 %copy.28 = f32[6,49,128]{2,1,0:T(8,128)} copy(f32[6,49,128]{2,1,0:T(8,128)S(1)} %get-tuple-element.3) | data formatting | bytes 301056

commit v2 on v1

--- a/solution.py
+++ b/solution.py
@@ -510,7 +510,7 @@
     table(0)
     table(1)
     each(fault_moves(0), "wait_recv")
-    weave(local(1), [functools.partial(arrived, k) for k in range(4)] + [functools.partial(near_pick, i) for i in range(4)])
+    weave(local(1), [functools.partial(arrived, k) for k in range(4)])
 
     each(fault_moves(1) + halo_moves, "wait_recv")
     arrived(4)
@@ -549,6 +549,7 @@
     each(back_moves, "start")
     br[own_list, :] = bs[own_list, :]
 
+    weave([functools.partial(near_pick, i) for i in range(4)])
     ht = hr[...].T
     for q in range(Q):
         full = dot(w2[3 * B :, :], split_rows(ht[q * B : (q + 1) * B, :]))

time: 30.3 us -> 29.8 us (0.983)
  Pallas kernels: 27.4 us -> 26.9 us
    pallas_call x1, Pallas kernels: 27.4 us -> 26.9 us  [per_device(): pl.pallas_call(functools.partial(kernel, n_group, n_dom), out_shape=(pltp...]
where the time goes in v2:
time: 29.8 us; the launch traced here: 29.6 us
  Pallas kernels  26.9 us (90%)
  local copies, waits for them, and re-layouts  1.46 us (5%)
  between operations  1.29 us (4%)
    pallas_call x1, Pallas kernels, per_device(): pl.pallas_call(functools.partial(kernel, n_group, n_dom), out_shape=(pltp...  26.9 us
    unnamed x2, local copies, waits for them, and re-layouts  1.46 us

profile of v2, /device:TPU:1, one launch (start us, length us, event | category | flops | bytes accessed | tf_op | source)
XLA Modules:
  0.0 29.6 jit_solution(658754752664564930)
XLA Ops:
  1.3 26.9 %ader_step.1 = (f32[9,56,256]{2,1,0:T(8,128)S(1)}, f32[6,49,128]{2,1,0:T(8,128)S(1)}) custom-call(f32[9,56,256]{2,1,0:T(8,128)} %refs_0_.1, f32[9,9,3,256]{3,2,1,0:T(4,128)} %bitcast.13, f32[3,56,56]{2,1,0:T(8,128)} %refs_2_.1, f32[3,56,56]{2,1,0:T(8,128)} %refs_3_.1, f32[9,9,4,256]{3,2,1,0:T(4,128)} %bitcast.14, f32[9,9,4,256]{3,2,1,0:T(4,128)} %bitcast.15, ...), custom_call_target="tpu_custom_call" | custom-call | tf_op jit(solution)/shard_map/ader_step/pallas_call | solution.py:645
  28.1 0.8 %copy.27 = f32[9,56,256]{2,1,0:T(8,128)} copy(f32[9,56,256]{2,1,0:T(8,128)S(1)} %get-tuple-element.2) | data formatting | bytes 1032192
  28.9 0.7 %copy.28 = f32[6,49,128]{2,1,0:T(8,128)} copy(f32[6,49,128]{2,1,0:T(8,128)S(1)} %get-tuple-element.3) | data formatting | bytes 301056
